TPU v7x, 32 devices: a whole 2x2x4 slice. The times are simulated.
32 devices in a mesh: grp: 4 (over z), seq: 8 (over y, x, core).
Axes of the slice: x: 2, y: 2, z: 4, core: 2. Of those that a mesh axis runs over, the one named last changes fastest.
Arguments:
- tokens: bfloat16 [2048, 2560], P('seq', 'grp'), may hold values from -6 to 6
- cotangent: bfloat16 [2048, 2560], P('seq', 'grp'), may hold values from -3 to 3
- route_ids: int32 [2048, 2], P('seq'), may hold values from 0 to 7, all different within a row; in each aligned block of 256 rows (0 to 255, 256 to 511, ...) at most 96 rows name the same one
- route_weights: bfloat16 [2048, 2], P('seq'), may hold values from 0.099609375 to 1
- reset_steps: int32 [128], P('seq'), may hold values from 0 to 3
- decay: float32 [8, 2048], P('seq', 'grp'), may hold values from 0.2 to 0.9
- w_up: bfloat16 [8, 2560, 2048], P('seq', None, 'grp'), may hold values from -0.15625 to 0.15625
- w_down: bfloat16 [8, 2048, 2560], P('seq', 'grp'), may hold values from -0.125 to 0.125
Outputs:
- grad_x: bfloat16 [2048, 2560], P('seq', 'grp')
- grad_route: float32 [2048, 2], P('seq')
- grad_up: bfloat16 [8, 2560, 2048], P('seq', None, 'grp')
- grad_down: bfloat16 [8, 2048, 2560], P('seq', 'grp')
Inputs may be any that keep to these rules, and one draw needn't show every extreme that they name: `route_ids`: each token names two different experts. Within the 256 tokens of one index of seq no expert is named more than 96 times, and in some such blocks an expert is named exactly 96 times.
All inputs are finite; a program needn't handle non-finite values.
Results may differ from a plain program's by a relative error of at most 0.012.
Values may be sent and summed in bfloat16 or wider, within the bound.
A program may use at most 128 MiB of HBM per device.

v0:
```python
import jax
import jax.numpy as jnp
from jax import lax
from jax.sharding import PartitionSpec as P

STEPS = 4
RB = 16


SHARP = 4.0


def lif_rates(current, decay, resets):
    membrane = jnp.zeros_like(current)
    rate_sum = jnp.zeros_like(current)
    for step_index in range(STEPS):
        keep_mask = (resets != step_index).astype(jnp.float32)[:, None]
        membrane = keep_mask * decay[None, :] * membrane + current
        spike_now = jax.nn.sigmoid(SHARP * (membrane - 1.0))
        membrane = membrane - spike_now
        rate_sum = rate_sum + spike_now
    return rate_sum / STEPS


def body(tokens, cotangent, route_ids, route_weights, reset_steps, decay, w_up, w_down):
    token_count = tokens.shape[0]
    feat_cols = tokens.shape[1]
    experts = lax.axis_size("seq")
    full_width = feat_cols * lax.axis_size("grp")
    capacity = 3 * token_count // experts
    slot_count = experts * capacity
    pair_expert = route_ids.reshape(-1)
    pair_ids = jnp.arange(2 * token_count, dtype=jnp.int32)
    onehot = (pair_expert[:, None] == jnp.arange(experts, dtype=jnp.int32)[None, :]).astype(
        jnp.int32
    )
    position = jnp.sum((jnp.cumsum(onehot, 0) - onehot) * onehot, 1)
    slot_of_pair = pair_expert * capacity + position
    pair_of_slot = jnp.zeros((slot_count,), jnp.int32).at[slot_of_pair].set(pair_ids)
    filled = jnp.zeros((slot_count,), jnp.bfloat16).at[slot_of_pair].set(1)
    token_of_slot = pair_of_slot // 2
    slot_mask = filled[:, None]
    gate_slot = (route_weights.reshape(-1)[pair_of_slot] * filled).reshape(experts, capacity)
    reset_slot = (
        jnp.repeat(reset_steps, RB)[token_of_slot].astype(jnp.bfloat16).reshape(experts, capacity)
    )
    whole_x, whole_dy = (
        lax.all_gather(tokens, "grp", axis=1, tiled=True),
        lax.all_gather(cotangent, "grp", axis=1, tiled=True),
    )
    send_x = (whole_x[token_of_slot] * slot_mask).reshape(experts, capacity, full_width)
    send_dy = (whole_dy[token_of_slot] * slot_mask).reshape(experts, capacity, full_width)
    panel_x, panel_dy, slot_gates, slot_resets = (
        lax.all_to_all(send_x, "seq", split_axis=0, concat_axis=0, tiled=True),
        lax.all_to_all(send_dy, "seq", split_axis=0, concat_axis=0, tiled=True),
        lax.all_to_all(gate_slot, "seq", split_axis=0, concat_axis=0, tiled=True),
        lax.all_to_all(reset_slot, "seq", split_axis=0, concat_axis=0, tiled=True),
    )
    panel_x = panel_x.reshape(slot_count, full_width)
    panel_dy = panel_dy.reshape(slot_count, full_width)
    gate_values = slot_gates.reshape(-1).astype(jnp.float32)
    resets = slot_resets.reshape(-1).astype(jnp.float32)
    up_local = w_up[0]
    down_local = w_down[0]
    decay_local = decay[0]
    current = jnp.dot(panel_x, up_local, preferred_element_type=jnp.float32)
    back_raw = lax.dot_general(
        panel_dy, down_local, (((1,), (1,)), ((), ())), preferred_element_type=jnp.float32
    )
    rate_values, pullback = jax.vjp(lambda drive: lif_rates(drive, decay_local, resets), current)
    rates_low = rate_values.astype(jnp.bfloat16)
    gate_part = jnp.sum(rates_low.astype(jnp.float32) * back_raw, 1)
    weighted = (rates_low.astype(jnp.float32) * gate_values[:, None]).astype(jnp.bfloat16)
    grad_down = lax.dot_general(
        weighted, panel_dy, (((0,), (0,)), ((), ())), preferred_element_type=jnp.float32
    ).astype(jnp.bfloat16)
    d_current = pullback(back_raw * gate_values[:, None])[0]
    d_low = d_current.astype(jnp.bfloat16)
    grad_up = lax.dot_general(
        panel_x, d_low, (((0,), (0,)), ((), ())), preferred_element_type=jnp.float32
    ).astype(jnp.bfloat16)
    input_rows = lax.psum_scatter(
        lax.dot_general(
            up_local, d_low, (((1,), (1,)), ((), ())), preferred_element_type=jnp.float32
        ).astype(jnp.bfloat16),
        "grp",
        scatter_dimension=0,
        tiled=True,
    ).astype(jnp.float32)
    gate_total = lax.psum(gate_part, "grp")
    back_x, back_gate = (
        lax.all_to_all(
            input_rows.reshape(feat_cols, experts, capacity).astype(jnp.bfloat16),
            "seq",
            split_axis=1,
            concat_axis=1,
            tiled=True,
        ).astype(jnp.float32),
        lax.all_to_all(
            gate_total.reshape(1, experts, capacity).astype(jnp.bfloat16),
            "seq",
            split_axis=1,
            concat_axis=1,
            tiled=True,
        ).astype(jnp.float32),
    )
    picked = back_x.reshape(feat_cols, slot_count)[:, slot_of_pair].reshape(
        feat_cols, token_count, 2
    )
    grad_x = jnp.sum(picked, 2).T.astype(jnp.bfloat16)
    grad_route = back_gate.reshape(-1)[slot_of_pair].reshape(token_count, 2)
    return (grad_x, grad_route, grad_up[None], grad_down[None])


def solution(mesh):
    in_specs = (
        P("seq", "grp"),
        P("seq", "grp"),
        P("seq", None),
        P("seq", None),
        P("seq"),
        P("seq", "grp"),
        P("seq", None, "grp"),
        P("seq", "grp", None),
    )
    out_specs = (P("seq", "grp"), P("seq", None), P("seq", None, "grp"), P("seq", "grp", None))
    return jax.shard_map(body, mesh=mesh, in_specs=in_specs, out_specs=out_specs, check_vma=False)
```

profile of v0, /device:TPU:0, one launch (start us, length us, event | category | flops | bytes accessed | tf_op | source)
XLA Modules:
  0.0 331.5 jit_solution(9014168082047829677)
XLA Ops:
  7.2 0.7 all-gather.3.cloned.1.call-update
  8.0 0.7 all-gather.5.cloned.1.call-update
  8.7 0.8 copy.25
  9.5 0.1 eq.29
  9.6 0.1 eq.25
  9.8 1.1 reduce-window.6
  10.9 0.2 slice_reduce_fusion
  11.2 0.7 broadcast_multiply_fusion.2
  11.9 0.1 copy.24
  12.0 0.1 mul.176
  12.2 0.8 copy.27
  13.0 0.2 reshape.188
  13.3 2.4 scatter_custom_fusion
  15.7 3.8 %scatter_custom_fusion.1 = bf16[768]{0:T(1024)(128)(2,1)S(1)} fusion(s32[512]{0:T(512)S(1)} %bitcast.56, bf16[512]{0:T(512)(128)(2,1)S(1)} %broadcast.108, bf16[]{:T(256)} %constant.44.clone.1), kind=kCustom, calls=%fused_computation.96 | custom fusion | bytes 1538 | tf_op jit(solution)/shard_map/scatter | solution.py:40
  19.5 5.0 %gather_fusion.1 = bf16[768]{0:T(1024)(128)(2,1)S(1)} fusion(bf16[512]{0:T(512)(128)(2,1)S(1)} %reshape.188, s32[1024]{0:T(1024)S(1)} %pad_clamp_fusion.1), kind=kCustom, calls=%fused_computation.1 | custom fusion | bytes 6144 | tf_op jit(solution)/shard_map/gather | solution.py:43
  24.6 0.7 all_to_all.29
  25.2 5.2 %all-to-all-start.1 = ((bf16[8,1,96]{2,1,0:T(2,128)(2,1)}), bf16[8,1,96]{2,1,0:T(2,128)(2,1)S(1)}, u32[]{:S(2)}, u32[]{:S(2)}) async-start(bf16[8,1,96]{2,1,0:T(2,128)(2,1)} %all_to_all.29), calls=%async_computation.1 | async-start | bytes 8192 | tf_op jit(solution)/shard_map/all_to_all | solution.py:56
  30.7 5.0 %gather_fusion.2 = s32[768]{0:T(1024)S(1)} fusion(s32[256]{0:T(256)S(1)} %reshape.189, s32[1024]{0:T(1024)S(1)} %pad_clamp_fusion.2), kind=kCustom, calls=%fused_computation.2 | custom fusion | bytes 9216 | tf_op jit(solution)/shard_map/gather | solution.py:45
  35.7 0.7 convert_element_type.173
  36.3 8.3 %all-gather.3.cloned.1.call-done = bf16[256,2560]{1,0:T(8,128)(2,1)} async-done(((bf16[256,640]{1,0:T(8,128)(2,1)}), bf16[256,2560]{1,0:T(8,128)(2,1)}) %all-gather.3.cloned.1.call-update) | async-done | bytes 1310736 | tf_op jit(solution)/shard_map/all_gather | solution.py:49
  44.6 9.9 %gather_fusion = bf16[768,2560]{1,0:T(8,128)(2,1)} fusion(bf16[256,2560]{1,0:T(8,128)(2,1)} %all-gather.3.cloned.1.call-done, s32[1024]{0:T(1024)S(1)} %pad_clamp_fusion.2), kind=kCustom, calls=%fused_computation | custom fusion | bytes 7867392 | tf_op jit(solution)/shard_map/gather | solution.py:52
  54.5 23.5 %all-gather.5.cloned.1.call-done = bf16[256,2560]{1,0:T(8,128)(2,1)} async-done(((bf16[256,640]{1,0:T(8,128)(2,1)}), bf16[256,2560]{1,0:T(8,128)(2,1)}) %all-gather.5.cloned.1.call-update) | async-done | bytes 1310736 | tf_op jit(solution)/shard_map/all_gather | solution.py:48
  77.9 9.8 %gather_fusion.3 = bf16[768,2560]{1,0:T(8,128)(2,1)} fusion(bf16[256,2560]{1,0:T(8,128)(2,1)} %all-gather.5.cloned.1.call-done, s32[1024]{0:T(1024)S(1)} %pad_clamp_fusion.2), kind=kCustom, calls=%fused_computation.3 | custom fusion | bytes 7867392 | tf_op jit(solution)/shard_map/gather | solution.py:51
  87.8 3.7 %all-to-all-start.2 = ((bf16[8,1,96]{2,1,0:T(2,128)(2,1)}), bf16[8,1,96]{2,1,0:T(2,128)(2,1)S(1)}, u32[]{:S(2)}, u32[]{:S(2)}) async-start(bf16[8,1,96]{2,1,0:T(2,128)(2,1)} %convert_element_type.173), calls=%async_computation.2 | async-start | bytes 8192 | tf_op jit(solution)/shard_map/all_to_all | solution.py:57
  91.4 5.5 %broadcast_multiply_fusion = (bf16[8,96,2560]{2,1,0:T(8,128)(2,1)}, bf16[8,96,2560]{2,1,0:T(8,128)(2,1)}) fusion(bf16[8,96,2560]{2,1,0:T(8,128)(2,1)} %bitcast.49, bf16[8,96]{1,0:T(8,128)(2,1)S(1)} %mul.178, bf16[8,96,2560]{2,1,0:T(8,128)(2,1)} %bitcast.48), kind=kLoop, calls=%fused_computation.31 | loop fusion | flops 3932160 | bytes 15730176 | tf_op jit(solution)/shard_map/mul | solution.py:51
  96.9 50.8 %all_to_all.36 = bf16[8,96,2560]{2,1,0:T(8,128)(2,1)} all-to-all(bf16[8,96,2560]{2,1,0:T(8,128)(2,1)} %get-tuple-element.25), channel_id=1, replica_groups=mesh['grp'=4,'seq'=8] {'seq'}, dimensions={0} | all-to-all | bytes 7864320 | tf_op jit(solution)/shard_map/all_to_all | solution.py:54
  147.7 4.5 %all-to-all-start = ((bf16[8,96,2560]{2,1,0:T(8,128)(2,1)}), bf16[8,96,2560]{2,1,0:T(8,128)(2,1)}, u32[]{:S(2)}, u32[]{:S(2)}) async-start(bf16[8,96,2560]{2,1,0:T(8,128)(2,1)} %get-tuple-element.26), calls=%async_computation | async-start | bytes 7864320 | tf_op jit(solution)/shard_map/all_to_all | solution.py:55
  152.7 5.5 %fusion.4 = f32[768,512]{0,1:T(8,128)} fusion(bf16[768,2560]{1,0:T(8,128)(2,1)} %bitcast.51, bf16[1,2560,512]{2,1,0:T(8,128)(2,1)S(1)} %copy-done), kind=kOutput, calls=%fused_computation.15 | convolution fusion | flops 2013265920 | bytes 8126464 | tf_op jit(solution)/shard_map/dot_general | solution.py:66
  158.2 40.3 %all-to-all-done = bf16[8,96,2560]{2,1,0:T(8,128)(2,1)} async-done(((bf16[8,96,2560]{2,1,0:T(8,128)(2,1)}), bf16[8,96,2560]{2,1,0:T(8,128)(2,1)}, u32[]{:S(2)}, u32[]{:S(2)}) %all-to-all-start) | async-done | bytes 3932192 | tf_op jit(solution)/shard_map/all_to_all | solution.py:55
  198.5 9.1 %fusion.8 = (f32[768]{0:T(1024)S(1)}, bf16[768,512]{0,1:T(8,128)(2,1)S(1)}, bf16[768,512]{0,1:T(8,128)(2,1)S(1)}) fusion(f32[768,512]{0,1:T(8,128)} %fusion.4, f32[768]{0:T(1024)S(1)} %reshape.198, f32[768]{0:T(1024)S(1)} %reshape.199, f32[768]{0:T(1024)S(1)} %reshape.200, f32[512]{0:T(512)S(1)} %bitcast.59, f32[768]{0:T(1024)S(1)} %reshape.201, ...), kind=kOutput, calls=%fused_computation.33 | convolution fusion | flops 2043542784 | bytes 9719808 | tf_op jit(solution)/shard_map/dot_general | solution.py:67
  207.6 0.9 copy-done.3
  208.5 4.2 %fusion = bf16[2560,768]{0,1:T(8,128)(2,1)} fusion(bf16[768,512]{0,1:T(8,128)(2,1)S(1)} %get-tuple-element.22, bf16[1,2560,512]{2,1,0:T(8,128)(2,1)S(1)} %copy-done), kind=kOutput, calls=%fused_computation.9 | convolution fusion | flops 2015232000 | bytes 7340032 | tf_op jit(solution)/shard_map/dot_general | solution.py:83
  212.7 6.3 %copy.32 = bf16[2560,768]{1,0:T(8,128)(2,1)} copy(bf16[2560,768]{0,1:T(8,128)(2,1)} %fusion) | data formatting | bytes 7864320
  219.0 10.4 %psum.7 = bf16[768]{0:T(1024)(128)(2,1)S(1)} all-reduce(f32[768]{0:T(1024)S(1)} %get-tuple-element.20), channel_id=1, replica_groups=mesh['grp'=4,'seq'=8] {'grp'}, use_global_device_ids=true, to_apply=%region_8.9 | all-reduce | flops 768 | bytes 4608 | tf_op jit(solution)/shard_map/psum | solution.py:90
  229.4 0.7 convert_element_type.174
  230.1 3.3 all-to-all-start.5
  233.4 56.1 %reduce-scatter.4.cloned.1.call-done = bf16[640,768]{1,0:T(8,128)(2,1)} async-done(((bf16[2560,768]{1,0:T(8,128)(2,1)}), bf16[640,768]{1,0:T(8,128)(2,1)}) %reduce-scatter.4.cloned.1.call-update) | async-done | bytes 983056
  289.5 2.3 copy.33
  291.8 4.4 %all-to-all-start.4 = ((bf16[640,8,96]{0,2,1:T(8,128)(2,1)}), bf16[640,8,96]{0,2,1:T(8,128)(2,1)}, u32[]{:S(2)}, u32[]{:S(2)}) async-start(bf16[640,8,96]{0,2,1:T(8,128)(2,1)} %bitcast.53), calls=%async_computation.4 | async-start | bytes 1966080 | tf_op jit(solution)/shard_map/all_to_all | solution.py:92
  296.3 6.1 %fusion.1 = bf16[1,2560,512]{2,1,0:T(8,128)(2,1)} fusion(bf16[768,2560]{1,0:T(8,128)(2,1)} %bitcast.52, bf16[768,512]{0,1:T(8,128)(2,1)} %copy-done.3), kind=kOutput, calls=%fused_computation.12 | convolution fusion | flops 2014576640 | bytes 7340032 | tf_op jit(solution)/shard_map/dot_general | solution.py:79
  302.3 5.8 %fusion.2 = bf16[1,512,2560]{2,1,0:T(8,128)(2,1)} fusion(bf16[768,2560]{1,0:T(8,128)(2,1)} %bitcast.5, bf16[768,512]{0,1:T(8,128)(2,1)S(1)} %get-tuple-element.21, f32[768]{0:T(1024)S(1)} %reshape.197), kind=kOutput, calls=%fused_computation.13 | convolution fusion | flops 2015756288 | bytes 7343104 | tf_op jit(solution)/shard_map/dot_general | solution.py:74
  308.2 2.3 gather_fusion.5
  310.5 0.1 reshape.196
  310.7 0.7 copy.31
  311.3 2.6 bitcast_convert_fusion
  314.0 4.5 %gather_fusion.4 = f32[512,640]{1,0:T(8,128)} fusion(f32[640,768]{0,1:T(8,128)} %bitcast_convert_fusion, s32[1024]{0:T(1024)S(1)} %pad_clamp_fusion), kind=kCustom, calls=%fused_computation.4 | custom fusion | bytes 2623488 | tf_op jit(solution)/shard_map/gather | solution.py:107
  318.4 2.9 reshape.193
  321.3 3.6 %reduce_sum.31 = bf16[640,256]{0,1:T(8,128)(2,1)} reduce(f32[640,256,2]{0,2,1:T(2,128)} %reshape.193, f32[]{:T(128)} %constant.51.clone.1), dimensions={2}, to_apply=%region_6.7 | reduce | flops 163840 | bytes 1638404 | tf_op jit(solution)/shard_map/reduce_sum | solution.py:110
  (40 shorter events, 1.1 us)
Async XLA Ops:
  7.2 145.5 %copy-start = (bf16[1,2560,512]{2,1,0:T(8,128)(2,1)S(1)}, bf16[1,2560,512]{2,1,0:T(8,128)(2,1)}, u32[]{:S(2)}) copy-start(bf16[1,2560,512]{2,1,0:T(8,128)(2,1)} %param.14) | copy-start | bytes 7864324
  7.2 37.4 %all-gather.3.cloned.1.call-start = ((), (), s32[]{:S(2)}) async-start(), calls=%async_computation.7 | async-start | bytes 1638400 | tf_op jit(solution)/shard_map/all_gather | solution.py:49
  7.9 70.0 %all-gather.5.cloned.1.call-start = ((), (), s32[]{:S(2)}) async-start(), calls=%async_computation.8 | async-start | bytes 1638400 | tf_op jit(solution)/shard_map/all_gather | solution.py:48
  8.7 21.8 %copy-start.1 = (s32[16]{0:T(128)S(1)}, s32[16]{0:T(128)}, u32[]{:S(2)}) copy-start(s32[16]{0:T(128)} %param.12) | copy-start | bytes 196
  25.2 62.5 %all-to-all-start.1 = ((bf16[8,1,96]{2,1,0:T(2,128)(2,1)}), bf16[8,1,96]{2,1,0:T(2,128)(2,1)S(1)}, u32[]{:S(2)}, u32[]{:S(2)}) async-start(bf16[8,1,96]{2,1,0:T(2,128)(2,1)} %all_to_all.29), calls=%async_computation.1 | async-start | bytes 8192 | tf_op jit(solution)/shard_map/all_to_all | solution.py:56
  87.8 9.2 %all-to-all-start.2 = ((bf16[8,1,96]{2,1,0:T(2,128)(2,1)}), bf16[8,1,96]{2,1,0:T(2,128)(2,1)S(1)}, u32[]{:S(2)}, u32[]{:S(2)}) async-start(bf16[8,1,96]{2,1,0:T(2,128)(2,1)} %convert_element_type.173), calls=%async_computation.2 | async-start | bytes 8192 | tf_op jit(solution)/shard_map/all_to_all | solution.py:57
  147.7 50.8 %all-to-all-start = ((bf16[8,96,2560]{2,1,0:T(8,128)(2,1)}), bf16[8,96,2560]{2,1,0:T(8,128)(2,1)}, u32[]{:S(2)}, u32[]{:S(2)}) async-start(bf16[8,96,2560]{2,1,0:T(8,128)(2,1)} %get-tuple-element.26), calls=%async_computation | async-start | bytes 7864320 | tf_op jit(solution)/shard_map/all_to_all | solution.py:55
  152.2 137.3 %reduce-scatter.4.cloned.1.call-start = ((), (), s32[]{:S(2)}) async-start(), calls=%async_computation.9 | async-start | bytes 4915200
  152.7 45.8 %copy-start.2 = (f32[1,512]{1,0:T(1,128)S(1)}, f32[1,512]{1,0:T(1,128)}, u32[]{:S(2)}) copy-start(f32[1,512]{1,0:T(1,128)} %param.13) | copy-start | bytes 6148
  207.6 0.9 copy-start.3
  230.1 61.7 %all-to-all-start.5 = ((bf16[1,8,96]{2,0,1:T(2,128)(2,1)}), bf16[1,8,96]{2,0,1:T(2,128)(2,1)S(1)}, u32[]{:S(2)}, u32[]{:S(2)}) async-start(bf16[1,8,96]{2,0,1:T(2,128)(2,1)} %convert_element_type.174), calls=%async_computation.5 | async-start | bytes 8192 | tf_op jit(solution)/shard_map/all_to_all | solution.py:99
  291.8 19.5 %all-to-all-start.4 = ((bf16[640,8,96]{0,2,1:T(8,128)(2,1)}), bf16[640,8,96]{0,2,1:T(8,128)(2,1)}, u32[]{:S(2)}, u32[]{:S(2)}) async-start(bf16[640,8,96]{0,2,1:T(8,128)(2,1)} %bitcast.53), calls=%async_computation.4 | async-start | bytes 1966080 | tf_op jit(solution)/shard_map/all_to_all | solution.py:92
Sparse Core Ops, SparseCore 0:
  9.6 34.9 all-gather.2
  46.2 31.6 all-gather.4
  219.1 70.3 reduce-scatter.3
where the time goes:
time: 332 us
  waiting for transfers between devices  130 us (39%)
  local copies, waits for them, and re-layouts  61.1 us (18%)
  blocking collectives  61.1 us (18%)
  matrix products  30.7 us (9%)
  starting transfers between devices  21.2 us (6%)
  between operations  14 us (4%)
  other arithmetic  13.8 us (4%)
    unnamed x4, waiting for transfers between devices  57.5 us
    all_to_all x1, blocking collectives, body(): lax.all_to_all(send_x, 'seq', split_axis=0, concat_axis=0, tiled=True)  50.8 us
    all_to_all x1, waiting for transfers between devices, body(): lax.all_to_all(send_dy, 'seq', split_axis=0, concat_axis=0, tiled=True)  40.3 us
    all_gather x1, waiting for transfers between devices, body(): lax.all_gather(tokens, 'grp', axis=1, tiled=True)  23.5 us
    unnamed x13, local copies, waits for them, and re-layouts  11.7 us
    psum x1, blocking collectives, body(): gate_total = lax.psum(gate_part, 'grp')  10.4 us
    gather x1, local copies, waits for them, and re-layouts, body(): whole_dy[token_of_slot] * slot_mask  9.85 us
    gather x1, local copies, waits for them, and re-layouts, body(): whole_x[token_of_slot] * slot_mask  9.82 us
  transfers between devices with their start and end apart: 8, of which 4 were waited for; matrix products, arithmetic and copies ran while one was open for 21% of the time, Pallas kernels for 0%

commit v1 on v0

--- a/solution.py
+++ b/solution.py
@@ -1,6 +1,10 @@
+import functools
+
 import jax
 import jax.numpy as jnp
 from jax import lax
+from jax.experimental import pallas as pl
+from jax.experimental.pallas import tpu as pltpu
 from jax.sharding import PartitionSpec as P
 
 STEPS = 4
@@ -22,7 +26,7 @@
     return rate_sum / STEPS
 
 
-def body(tokens, cotangent, route_ids, route_weights, reset_steps, decay, w_up, w_down):
+def plain_body(tokens, cotangent, route_ids, route_weights, reset_steps, decay, w_up, w_down):
     token_count = tokens.shape[0]
     feat_cols = tokens.shape[1]
     experts = lax.axis_size("seq")
@@ -34,7 +38,9 @@
     onehot = (pair_expert[:, None] == jnp.arange(experts, dtype=jnp.int32)[None, :]).astype(
         jnp.int32
     )
-    position = jnp.sum((jnp.cumsum(onehot, 0) - onehot) * onehot, 1)
+    before = jnp.tril(jnp.ones((2 * token_count, 2 * token_count), jnp.bfloat16), -1)
+    counts = jnp.dot(before, onehot.astype(jnp.bfloat16), preferred_element_type=jnp.float32)
+    position = jnp.sum(counts.astype(jnp.int32) * onehot, 1)
     slot_of_pair = pair_expert * capacity + position
     pair_of_slot = jnp.zeros((slot_count,), jnp.int32).at[slot_of_pair].set(pair_ids)
     filled = jnp.zeros((slot_count,), jnp.bfloat16).at[slot_of_pair].set(1)
@@ -112,6 +118,381 @@
     return (grad_x, grad_route, grad_up[None], grad_down[None])
 
 
+MESH = pl.DeviceIdType.MESH
+F32 = jnp.float32
+BF16 = jnp.bfloat16
+
+
+def flip(index, other, count):
+    total, bit = 0, 1
+    while bit < count:
+        total = total + bit * ((index // bit + other // bit) % 2)
+        bit *= 2
+    return total
+
+
+def nt_dot(a, b):
+    return lax.dot_general(a, b, (((1,), (1,)), ((), ())), preferred_element_type=F32)
+
+
+def tn_dot(a, b):
+    return lax.dot_general(a, b, (((0,), (0,)), ((), ())), preferred_element_type=F32)
+
+
+def moe_kernel(
+    n_grp, n_seq,
+    tok, cot, info, slot_cols, decay, up_hbm, down_hbm,
+    gx_out, gr_out, gu_out, gd_out,
+    up, down, zbuf, gmat, gmat_t, send, recv, msend, mrecv, cur, raw, wgt, dlow,
+    rsend, rrecv, gsend, grecv, zsend, zrecv, own, row_send, row_recv, gu, gd,
+    zs, zr, ds, dr, ms, mr, rs, rr, gs, gr, zbs, zbr, rws, rwr, local,
+):
+    z = lax.axis_index("grp")
+    s = lax.axis_index("seq")
+    tokens, width = tok.shape
+    cap = recv.shape[3]
+    slots = n_seq * cap
+    hidden = up.shape[1]
+
+    def z_copy(source, target, send_sem, recv_sem, o):
+        return pltpu.make_async_remote_copy(
+            src_ref=source, dst_ref=target, send_sem=send_sem, recv_sem=recv_sem,
+            device_id=(flip(z, o, n_grp), s), device_id_type=MESH)
+
+    def s_copy(source, target, send_sem, recv_sem, o):
+        return pltpu.make_async_remote_copy(
+            src_ref=source, dst_ref=target, send_sem=send_sem, recv_sem=recv_sem,
+            device_id=(z, flip(s, o, n_seq)), device_id_type=MESH)
+
+    load_up = pltpu.make_async_copy(up_hbm, up, local.at[0])
+    load_down = pltpu.make_async_copy(down_hbm, down, local.at[1])
+    load_up.start()
+    load_down.start()
+
+    barrier = pltpu.get_barrier_semaphore()
+    for o in range(1, n_grp):
+        pl.semaphore_signal(barrier, inc=1, device_id=(flip(z, o, n_grp), s), device_id_type=MESH)
+    for o in range(1, n_seq):
+        pl.semaphore_signal(barrier, inc=1, device_id=(z, flip(s, o, n_seq)), device_id_type=MESH)
+    pl.semaphore_wait(barrier, n_grp + n_seq - 2)
+
+    x_copies, y_copies = [None], [None]
+    for o in range(1, n_grp):
+        x_copies.append(z_copy(tok, zbuf.at[o, 0], zs.at[o, 0], zr.at[o, 0], o))
+        y_copies.append(z_copy(cot, zbuf.at[o, 1], zs.at[o, 1], zr.at[o, 1], o))
+        x_copies[o].start()
+        y_copies[o].start()
+
+    lane = lax.broadcasted_iota(jnp.int32, (cap, 128), 1)
+    row_id = lax.broadcasted_iota(jnp.int32, (cap, tokens), 0)
+
+    def hits(o):
+        ids = (row_id + o * cap).astype(F32)
+        return ids == info[0:1, :], ids == info[1:2, :]
+
+    def prepare(o, carry):
+        first, second = hits(o)
+        either = jnp.where(first, 1.0, jnp.where(second, 1.0, 0.0))
+        gmat[o] = either.astype(BF16)
+        gate = jnp.sum(
+            jnp.where(first, info[2:3, :], jnp.where(second, info[3:4, :], 0.0)), 1, keepdims=True)
+        reset = jnp.sum(either * info[4:5, :], 1, keepdims=True)
+        msend[o] = jnp.where(lane == 0, gate, reset)
+        return carry
+
+    lax.fori_loop(0, n_seq, prepare, 0)
+
+    def dispatch(stage, x_ref, y_ref):
+        def one(o, carry):
+            send[stage, o, 0] = jnp.dot(
+                gmat[o], x_ref[...], preferred_element_type=F32).astype(BF16)
+            send[stage, o, 1] = jnp.dot(
+                gmat[o], y_ref[...], preferred_element_type=F32).astype(BF16)
+            s_copy(send.at[stage, o], recv.at[stage, o], ds.at[stage, o], dr.at[stage, o], o).start()
+            return carry
+
+        lax.fori_loop(1, n_seq, one, 0)
+        recv[stage, 0, 0] = jnp.dot(gmat[0], x_ref[...], preferred_element_type=F32).astype(BF16)
+        recv[stage, 0, 1] = jnp.dot(gmat[0], y_ref[...], preferred_element_type=F32).astype(BF16)
+
+    dispatch(0, tok, cot)
+    for o in range(1, n_seq):
+        s_copy(msend.at[o], mrecv.at[o], ms.at[o], mr.at[o], o).start()
+    mrecv[0] = msend[0]
+    col_id = lax.broadcasted_iota(jnp.int32, (tokens, slots), 1).astype(F32)
+    gmat_t[...] = jnp.where(
+        col_id == slot_cols[:, 0:1], 1.0, jnp.where(col_id == slot_cols[:, 1:2], 1.0, 0.0)
+    ).astype(BF16)
+    for o in range(1, n_grp):
+        x_copies[o].wait_recv()
+        y_copies[o].wait_recv()
+        dispatch(o, zbuf.at[o, 0], zbuf.at[o, 1])
+
+    load_up.wait()
+    load_down.wait()
+    cur[...] = jnp.zeros_like(cur)
+    raw[...] = jnp.zeros_like(raw)
+    tile = min(hidden, 256)
+
+    def slice_at(stage):
+        return pl.multiple_of(flip(z, stage, n_grp) * width, width)
+
+    def forward(stage, carry):
+        def arrive(o, inner):
+            s_copy(send.at[stage, o], recv.at[stage, o], ds.at[stage, o], dr.at[stage, o], o).wait_recv()
+            return inner
+
+        lax.fori_loop(1, n_seq, arrive, 0)
+        base = slice_at(stage)
+
+        def columns(n, inner):
+            at = pl.multiple_of(n * tile, tile)
+            x = recv[stage, :, 0].reshape(slots, width)
+            cur[:, pl.ds(at, tile)] += jnp.dot(
+                x, up[pl.ds(base, width), pl.ds(at, tile)], preferred_element_type=F32)
+            y = recv[stage, :, 1].reshape(slots, width)
+            raw[:, pl.ds(at, tile)] += nt_dot(y, down[pl.ds(at, tile), pl.ds(base, width)])
+            return inner
+
+        lax.fori_loop(0, hidden // tile, columns, 0)
+        return carry
+
+    lax.fori_loop(0, n_grp, forward, 0)
+    for o in range(1, n_seq):
+        s_copy(msend.at[o], mrecv.at[o], ms.at[o], mr.at[o], o).wait_recv()
+
+    rows = 16
+
+    def neurons(o, carry):
+        def part(i, inner):
+            at = pl.multiple_of(o * cap + i * rows, rows)
+            here = pl.multiple_of(i * rows, rows)
+            drive = cur[pl.ds(at, rows), :]
+            back = raw[pl.ds(at, rows), :]
+            gate = mrecv[o, pl.ds(here, rows), 0:1]
+            reset = mrecv[o, pl.ds(here, rows), 1:2]
+            leak = decay[0:1, :]
+            spikes, scales = [], []
+            membrane = None
+            for step in range(STEPS):
+                if step == 0:
+                    membrane = drive
+                    scales.append(None)
+                else:
+                    keep = jnp.where(reset == float(step), 0.0, 1.0)
+                    scale = keep * leak
+                    scales.append(scale)
+                    membrane = scale * membrane + drive
+                spike = jax.nn.sigmoid(SHARP * (membrane - 1.0))
+                membrane = membrane - spike
+                spikes.append(spike)
+            rate = ((spikes[0] + spikes[1] + spikes[2] + spikes[3]) / STEPS).astype(BF16).astype(F32)
+            total = jnp.sum(rate * back, 1, keepdims=True)
+            gsend[o, pl.ds(here, rows), :] = jnp.broadcast_to(total, (rows, 128))
+            wgt[pl.ds(at, rows), :] = (rate * gate).astype(BF16)
+            upstream = back * gate / STEPS
+            d_v, d_cur = None, None
+            for step in reversed(range(STEPS)):
+                spike = spikes[step]
+                slope = SHARP * spike * (1.0 - spike)
+                if d_v is None:
+                    d_m = upstream * slope
+                    d_cur = d_m
+                else:
+                    d_m = d_v + (upstream - d_v) * slope
+                    d_cur = d_cur + d_m
+                if step > 0:
+                    d_v = scales[step] * d_m
+            dlow[pl.ds(at, rows), :] = d_cur.astype(BF16)
+            return inner
+
+        lax.fori_loop(0, cap // rows, part, 0)
+        return carry
+
+    lax.fori_loop(0, n_seq, neurons, 0)
+
+    for o in range(1, n_seq):
+        s_copy(gsend.at[o], grecv.at[o], gs.at[o], gr.at[o], o).start()
+    grecv[0] = gsend[0]
+
+    half = n_seq // 2
+
+    def give_back(turn, carry):
+        stage = n_grp - 1 - turn
+        base = slice_at(stage)
+
+        def block(h, inner):
+            at = pl.multiple_of(h * half * cap, half * cap)
+            value = nt_dot(dlow[pl.ds(at, half * cap), :], up[pl.ds(base, width), :]).astype(BF16)
+            rsend[stage, pl.ds(h * half, half)] = value.reshape(half, cap, width)
+            return inner
+
+        lax.fori_loop(0, 2, block, 0)
+        rrecv[stage, 0] = rsend[stage, 0]
+
+        def go(o, inner):
+            s_copy(rsend.at[stage, o], rrecv.at[stage, o], rs.at[stage, o], rr.at[stage, o], o).start()
+            return inner
+
+        lax.fori_loop(1, n_seq, go, 0)
+        return carry
+
+    lax.fori_loop(0, n_grp, give_back, 0)
+
+    def weight_grads(stage, carry):
+        base = slice_at(stage)
+        gu[pl.ds(base, width), :] = tn_dot(
+            recv[stage, :, 0].reshape(slots, width), dlow[...]).astype(BF16)
+        gd[:, pl.ds(base, width)] = tn_dot(
+            wgt[...], recv[stage, :, 1].reshape(slots, width)).astype(BF16)
+        return carry
+
+    lax.fori_loop(0, n_grp, weight_grads, 0)
+    store_up = pltpu.make_async_copy(gu, gu_out, local.at[2])
+    store_down = pltpu.make_async_copy(gd, gd_out, local.at[3])
+    store_up.start()
+    store_down.start()
+
+    for o in range(1, n_seq):
+        s_copy(gsend.at[o], grecv.at[o], gs.at[o], gr.at[o], o).wait_recv()
+
+    def route(o, carry):
+        first, second = hits(o)
+        gates = jnp.concatenate([grecv[o]] * (tokens // 128), axis=1)
+        return (
+            carry[0] + jnp.sum(jnp.where(first, gates, 0.0), 0, keepdims=True),
+            carry[1] + jnp.sum(jnp.where(second, gates, 0.0), 0, keepdims=True),
+        )
+
+    empty = jnp.zeros((1, tokens), F32)
+    route0, route1 = lax.fori_loop(0, n_seq, route, (empty, empty))
+    which = lax.broadcasted_iota(jnp.int32, (8, tokens), 0)
+    row_send[...] = jnp.where(which == 0, route0, route1)
+    row_copies = [None] + [
+        z_copy(row_send, row_recv.at[o], rws.at[o], rwr.at[o], o) for o in range(1, n_grp)]
+    for o in range(1, n_grp):
+        row_copies[o].start()
+
+    x_back = [None] + [
+        z_copy(zsend.at[o], zrecv.at[o], zbs.at[o], zbr.at[o], o) for o in range(1, n_grp)]
+    for stage in reversed(range(n_grp)):
+        for o in range(1, n_seq):
+            s_copy(rsend.at[stage, o], rrecv.at[stage, o], rs.at[stage, o], rr.at[stage, o], o).wait_recv()
+        value = jnp.dot(
+            gmat_t[...], rrecv[stage].reshape(slots, width), preferred_element_type=F32)
+        if stage > 0:
+            zsend[stage] = value.astype(BF16)
+            x_back[stage].start()
+        else:
+            own[...] = value
+    total_rows = row_send[...]
+    for o in range(1, n_grp):
+        row_copies[o].wait_recv()
+        total_rows = total_rows + row_recv[o]
+    gr_out[...] = total_rows
+    for o in reversed(range(1, n_grp)):
+        x_back[o].wait_recv()
+        own[...] += zrecv[o].astype(F32)
+    gx_out[...] = own[...].astype(BF16)
+
+    for o in range(1, n_grp):
+        x_copies[o].wait_send()
+        y_copies[o].wait_send()
+        row_copies[o].wait_send()
+        x_back[o].wait_send()
+
+    def finish(o, carry):
+        s_copy(msend.at[o], mrecv.at[o], ms.at[o], mr.at[o], o).wait_send()
+        s_copy(gsend.at[o], grecv.at[o], gs.at[o], gr.at[o], o).wait_send()
+
+        def each(stage, inner):
+            s_copy(send.at[stage, o], recv.at[stage, o], ds.at[stage, o], dr.at[stage, o], o).wait_send()
+            s_copy(rsend.at[stage, o], rrecv.at[stage, o], rs.at[stage, o], rr.at[stage, o], o).wait_send()
+            return inner
+
+        lax.fori_loop(0, n_grp, each, 0)
+        return carry
+
+    lax.fori_loop(1, n_seq, finish, 0)
+    store_up.wait()
+    store_down.wait()
+
+
+def body(tokens, cotangent, route_ids, route_weights, reset_steps, decay, w_up, w_down):
+    token_count, width = tokens.shape
+    n_grp, n_seq = lax.axis_size("grp"), lax.axis_size("seq")
+    cap = 3 * token_count // n_seq
+    slots = n_seq * cap
+    _, full, hidden = w_up.shape
+    if width % 128 or cap % 16 or hidden % 256 or token_count % 128 or n_grp & (n_grp - 1) or n_seq & (n_seq - 1):
+        return plain_body(
+            tokens, cotangent, route_ids, route_weights, reset_steps, decay, w_up, w_down)
+    experts = jnp.arange(n_seq, dtype=jnp.int32)
+    onehot = (route_ids[:, :, None] == experts[None, None, :]).astype(F32)
+    both = jnp.sum(onehot, 1).astype(BF16)
+    before = jnp.tril(jnp.ones((token_count, token_count), BF16), -1)
+    counts = jnp.dot(before, both, preferred_element_type=F32)
+    position = jnp.sum(counts[:, None, :] * onehot, 2)
+    block = (route_ids ^ lax.axis_index("seq")).astype(F32)
+    slot = block * cap + position
+    resets = jnp.repeat(reset_steps, RB).astype(F32)
+    info = jnp.concatenate(
+        [slot.T, route_weights.astype(F32).T, resets[None], jnp.zeros((3, token_count), F32)], 0)
+    slot_cols = slot
+    vmem = pl.BlockSpec(memory_space=pltpu.VMEM)
+    hbm = pl.BlockSpec(memory_space=pl.ANY)
+    dma = pltpu.SemaphoreType.DMA
+    panel = (n_grp, n_seq, cap, width)
+    grad_x, rows, grad_up, grad_down = pl.pallas_call(
+        functools.partial(moe_kernel, n_grp, n_seq),
+        out_shape=(
+            jax.ShapeDtypeStruct((token_count, width), BF16),
+            jax.ShapeDtypeStruct((8, token_count), F32),
+            jax.ShapeDtypeStruct((full, hidden), BF16),
+            jax.ShapeDtypeStruct((hidden, full), BF16),
+        ),
+        in_specs=[vmem, vmem, vmem, vmem, vmem, hbm, hbm],
+        out_specs=(vmem, vmem, hbm, hbm),
+        scratch_shapes=[
+            pltpu.VMEM((full, hidden), BF16),
+            pltpu.VMEM((hidden, full), BF16),
+            pltpu.VMEM((n_grp, 2, token_count, width), BF16),
+            pltpu.VMEM((n_seq, cap, token_count), BF16),
+            pltpu.VMEM((token_count, slots), BF16),
+            pltpu.VMEM((n_grp, n_seq, 2, cap, width), BF16),
+            pltpu.VMEM((n_grp, n_seq, 2, cap, width), BF16),
+            pltpu.VMEM((n_seq, cap, 128), F32),
+            pltpu.VMEM((n_seq, cap, 128), F32),
+            pltpu.VMEM((slots, hidden), F32),
+            pltpu.VMEM((slots, hidden), F32),
+            pltpu.VMEM((slots, hidden), BF16),
+            pltpu.VMEM((slots, hidden), BF16),
+            pltpu.VMEM(panel, BF16),
+            pltpu.VMEM(panel, BF16),
+            pltpu.VMEM((n_seq, cap, 128), F32),
+            pltpu.VMEM((n_seq, cap, 128), F32),
+            pltpu.VMEM((n_grp, token_count, width), BF16),
+            pltpu.VMEM((n_grp, token_count, width), BF16),
+            pltpu.VMEM((token_count, width), F32),
+            pltpu.VMEM((8, token_count), F32),
+            pltpu.VMEM((n_grp, 8, token_count), F32),
+            pltpu.VMEM((full, hidden), BF16),
+            pltpu.VMEM((hidden, full), BF16),
+            dma((n_grp, 2)), dma((n_grp, 2)),
+            dma((n_grp, n_seq)), dma((n_grp, n_seq)),
+            dma((n_seq,)), dma((n_seq,)),
+            dma((n_grp, n_seq)), dma((n_grp, n_seq)),
+            dma((n_seq,)), dma((n_seq,)),
+            dma((n_grp,)), dma((n_grp,)),
+            dma((n_grp,)), dma((n_grp,)),
+            dma((4,)),
+        ],
+        compiler_params=pltpu.CompilerParams(
+            collective_id=0, has_side_effects=True, vmem_limit_bytes=60 * 1024 * 1024),
+    )(tokens, cotangent, info, slot_cols, decay, w_up[0], w_down[0])
+    return grad_x, rows[:2].T, grad_up[None], grad_down[None]
+
+
 def solution(mesh):
     in_specs = (
         P("seq", "grp"),

time: 332 us -> 180 us (0.54)
  Pallas kernels: 0 us -> 166 us
  waiting for transfers between devices: 130 us -> 0 us
  blocking collectives: 61.1 us -> 0 us
  local copies, waits for them, and re-layouts: 61.1 us -> 9.31 us
  matrix products: 30.7 us -> 0.23 us
  starting transfers between devices: 21.2 us -> 0 us
  between operations: 14 us -> 0.68 us
  other arithmetic: 13.8 us -> 3.46 us
    pallas_call x0 -> x1, Pallas kernels: none -> 166 us  [body(): pl.pallas_call(functools.partial(moe_kernel, n_grp, n_seq), out_shape=(ja...]
    unnamed x4 -> x0, waiting for transfers between devices: 57.5 us -> none
    all_to_all x1 -> x0, blocking collectives: 50.8 us -> none  [body(): lax.all_to_all(send_x, 'seq', split_axis=0, concat_axis=0, tiled=True)]
    all_to_all x5 -> x0, waiting for transfers between devices: 40.3 us -> none  [the longest x1 40.3 us: body(): lax.all_to_all(send_dy, 'seq', split_axis=0, concat_axis=0, tiled=True)]
    gather x6 -> x0, local copies, waits for them, and re-layouts: 36.4 us -> none  [the longest x1 9.85 us: body(): whole_dy[token_of_slot] * slot_mask]
    all_gather x2 -> x0, waiting for transfers between devices: 31.7 us -> none  [the longest x1 23.5 us: body(): lax.all_gather(tokens, 'grp', axis=1, tiled=True)]
    dot_general x5 -> x1, matrix products: 30.7 us -> 0.23 us  [body(): counts = jnp.dot(before, both, preferred_element_type=F32)]
    all_to_all x5 -> x0, starting transfers between devices: 21.1 us -> none  [the longest x1 5.17 us: body(): lax.all_to_all(gate_slot, 'seq', split_axis=0, concat_axis=0, tiled=True)]
  transfers between devices with their start and end apart: 8 -> 0, of which waited for: 4 -> 0; matrix products, arithmetic and copies ran while one was open for 21% -> 0% of each run, Pallas kernels for 0% -> 0%
where the time goes in v1:
time: 180 us
  Pallas kernels  166 us (92%)
  local copies, waits for them, and re-layouts  9.31 us (5%)
  other arithmetic  3.46 us (2%)
    pallas_call x1, Pallas kernels, body(): pl.pallas_call(functools.partial(moe_kernel, n_grp, n_seq), out_shape=(ja...  166 us
    unnamed x8, local copies, waits for them, and re-layouts  7.59 us

profile of v1, /device:TPU:0, one launch (start us, length us, event | category | flops | bytes accessed | tf_op | source)
XLA Modules:
  0.0 179.8 jit_solution(242042123910939338)
XLA Ops:
  0.6 0.7 convert_element_type.27
  1.3 0.1 pad.3.clone
  1.4 0.7 convert_bitcast_fusion
  2.1 0.7 convert_reduce_fusion
  2.7 0.2 fusion.1
  3.0 0.7 select_reduce_fusion
  3.7 0.1 broadcast_in_dim.25
  3.8 0.1 convert_element_type.28
  3.9 0.1 copy.21
  4.0 0.8 copy.19
  4.8 0.0 copy-start.1
  4.9 0.1 copy.22
  4.9 0.7 maximum_maximum_fusion.info
  5.6 0.0 copy-done.1
  5.6 166.1 %shard_map.111 = (bf16[256,640]{1,0:T(8,128)(2,1)}, f32[8,256]{1,0:T(8,128)}, bf16[2560,512]{1,0:T(8,128)(2,1)}, bf16[512,2560]{1,0:T(8,128)(2,1)}) custom-call(bf16[256,640]{1,0:T(8,128)(2,1)} %tok.1, bf16[256,640]{1,0:T(8,128)(2,1)} %cot.1, f32[8,256]{1,0:T(8,128)} %maximum_maximum_fusion.info, f32[256,2]{1,0:T(8,128)} %copy-done.1, f32[1,512]{1,0:T(1,128)} %decay.1, ...), custom_call_target="tpu_custom_call" | custom-call | tf_op jit(solution)/shard_map/pallas_call | solution.py:446
  171.8 1.3 slice_bitcast_fusion
  173.0 1.7 copy.26
  174.8 0.0 copy-start
  174.8 3.6 %copy.27 = bf16[1,2560,512]{2,1,0:T(8,128)(2,1)} copy(bf16[1,2560,512]{2,1,0:T(8,128)(2,1)} %bitcast.13) | data formatting | bytes 5242880
  178.3 0.0 copy-done
  178.3 1.5 copy.28
  (3 shorter events, 0.0 us)
Async XLA Ops:
  4.8 0.8 copy-start.1
  174.8 3.6 %copy-start = (bf16[512,2560]{1,0:T(8,128)(2,1)S(1)}, bf16[512,2560]{1,0:T(8,128)(2,1)}, u32[]{:S(2)}) copy-start(bf16[512,2560]{1,0:T(8,128)(2,1)} %get-tuple-element.11) | copy-start | bytes 7864324

commit v2 on v1

--- a/solution.py
+++ b/solution.py
@@ -145,7 +145,7 @@
     gx_out, gr_out, gu_out, gd_out,
     up, down, zbuf, gmat, gmat_t, send, recv, msend, mrecv, cur, raw, wgt, dlow,
     rsend, rrecv, gsend, grecv, zsend, zrecv, own, row_send, row_recv, gu, gd,
-    zs, zr, ds, dr, ms, mr, rs, rr, gs, gr, zbs, zbr, rws, rwr, local,
+    zs, zr, ds, dr, ms, mr, rs, rr, gs, gr, zbs, zbr, rws, rwr, fs, fr, es, er, local,
 ):
     z = lax.axis_index("grp")
     s = lax.axis_index("seq")
@@ -176,12 +176,13 @@
         pl.semaphore_signal(barrier, inc=1, device_id=(z, flip(s, o, n_seq)), device_id_type=MESH)
     pl.semaphore_wait(barrier, n_grp + n_seq - 2)
 
-    x_copies, y_copies = [None], [None]
-    for o in range(1, n_grp):
-        x_copies.append(z_copy(tok, zbuf.at[o, 0], zs.at[o, 0], zr.at[o, 0], o))
-        y_copies.append(z_copy(cot, zbuf.at[o, 1], zs.at[o, 1], zr.at[o, 1], o))
-        x_copies[o].start()
-        y_copies[o].start()
+    far = [
+        z_copy(tok, zbuf.at[2, 0], zs.at[2, 0], zr.at[2, 0], 2),
+        z_copy(cot, zbuf.at[2, 1], zs.at[2, 1], zr.at[2, 1], 2),
+    ]
+    relay = [z_copy(zbuf.at[2, a], zbuf.at[3, a], zs.at[3, a], zr.at[3, a], 1) for a in (0, 1)]
+    for copy in far:
+        copy.start()
 
     lane = lax.broadcasted_iota(jnp.int32, (cap, 128), 1)
     row_id = lax.broadcasted_iota(jnp.int32, (cap, tokens), 0)
@@ -223,10 +224,25 @@
     gmat_t[...] = jnp.where(
         col_id == slot_cols[:, 0:1], 1.0, jnp.where(col_id == slot_cols[:, 1:2], 1.0, 0.0)
     ).astype(BF16)
-    for o in range(1, n_grp):
-        x_copies[o].wait_recv()
-        y_copies[o].wait_recv()
-        dispatch(o, zbuf.at[o, 0], zbuf.at[o, 1])
+
+    def pass_panel(o):
+        return z_copy(recv.at[0, o], recv.at[1, o], fs.at[o], fr.at[o], 1)
+
+    def pass_on(o, carry):
+        s_copy(send.at[0, o], recv.at[0, o], ds.at[0, o], dr.at[0, o], o).wait_recv()
+        pass_panel(o).start()
+        return carry
+
+    pass_panel(0).start()
+    lax.fori_loop(1, n_seq // 2, pass_on, 0)
+    for copy, onward in zip(far, relay):
+        copy.wait_recv()
+        onward.start()
+    dispatch(2, zbuf.at[2, 0], zbuf.at[2, 1])
+    lax.fori_loop(n_seq // 2, n_seq, pass_on, 0)
+    for onward in relay:
+        onward.wait_recv()
+    dispatch(3, zbuf.at[3, 0], zbuf.at[3, 1])
 
     load_up.wait()
     load_down.wait()
@@ -237,12 +253,18 @@
     def slice_at(stage):
         return pl.multiple_of(flip(z, stage, n_grp) * width, width)
 
-    def forward(stage, carry):
+    def forward(stage):
         def arrive(o, inner):
-            s_copy(send.at[stage, o], recv.at[stage, o], ds.at[stage, o], dr.at[stage, o], o).wait_recv()
+            if stage == 1:
+                pass_panel(o).wait_recv()
+            else:
+                s_copy(
+                    send.at[stage, o], recv.at[stage, o], ds.at[stage, o], dr.at[stage, o], o
+                ).wait_recv()
             return inner
 
-        lax.fori_loop(1, n_seq, arrive, 0)
+        if stage > 0:
+            lax.fori_loop(0 if stage == 1 else 1, n_seq, arrive, 0)
         base = slice_at(stage)
 
         def columns(n, inner):
@@ -255,9 +277,9 @@
             return inner
 
         lax.fori_loop(0, hidden // tile, columns, 0)
-        return carry
-
-    lax.fori_loop(0, n_grp, forward, 0)
+
+    for stage in (0, 2, 1, 3):
+        forward(stage)
     for o in range(1, n_seq):
         s_copy(msend.at[o], mrecv.at[o], ms.at[o], mr.at[o], o).wait_recv()
 
@@ -317,27 +339,36 @@
 
     half = n_seq // 2
 
-    def give_back(turn, carry):
-        stage = n_grp - 1 - turn
+    def to_partner(h):
+        part = pl.ds(h * half, half)
+        return z_copy(rsend.at[1, part], rrecv.at[1, part], es.at[h], er.at[h], 1)
+
+    def give_back(stage):
         base = slice_at(stage)
 
         def block(h, inner):
             at = pl.multiple_of(h * half * cap, half * cap)
-            value = nt_dot(dlow[pl.ds(at, half * cap), :], up[pl.ds(base, width), :]).astype(BF16)
-            rsend[stage, pl.ds(h * half, half)] = value.reshape(half, cap, width)
+            value = nt_dot(dlow[pl.ds(at, half * cap), :], up[pl.ds(base, width), :])
+            value = value.reshape(half, cap, width)
+            if stage == 0:
+                to_partner(h).wait_recv()
+                value = value + rrecv[1, pl.ds(h * half, half)].astype(F32)
+            rsend[stage, pl.ds(h * half, half)] = value.astype(BF16)
+            if stage == 1:
+                to_partner(h).start()
             return inner
-
-        lax.fori_loop(0, 2, block, 0)
-        rrecv[stage, 0] = rsend[stage, 0]
 
         def go(o, inner):
             s_copy(rsend.at[stage, o], rrecv.at[stage, o], rs.at[stage, o], rr.at[stage, o], o).start()
             return inner
 
-        lax.fori_loop(1, n_seq, go, 0)
-        return carry
-
-    lax.fori_loop(0, n_grp, give_back, 0)
+        lax.fori_loop(0, 2, block, 0)
+        if stage != 1:
+            rrecv[stage, 0] = rsend[stage, 0]
+            lax.fori_loop(1, n_seq, go, 0)
+
+    for stage in (1, 3, 2):
+        give_back(stage)
 
     def weight_grads(stage, carry):
         base = slice_at(stage)
@@ -348,6 +379,7 @@
         return carry
 
     lax.fori_loop(0, n_grp, weight_grads, 0)
+    give_back(0)
     store_up = pltpu.make_async_copy(gu, gu_out, local.at[2])
     store_down = pltpu.make_async_copy(gd, gd_out, local.at[3])
     store_up.start()
@@ -373,9 +405,8 @@
     for o in range(1, n_grp):
         row_copies[o].start()
 
-    x_back = [None] + [
-        z_copy(zsend.at[o], zrecv.at[o], zbs.at[o], zbr.at[o], o) for o in range(1, n_grp)]
-    for stage in reversed(range(n_grp)):
+    x_back = {o: z_copy(zsend.at[o], zrecv.at[o], zbs.at[o], zbr.at[o], o) for o in (2, 3)}
+    for stage in (3, 2, 0):
         for o in range(1, n_seq):
             s_copy(rsend.at[stage, o], rrecv.at[stage, o], rs.at[stage, o], rr.at[stage, o], o).wait_recv()
         value = jnp.dot(
@@ -390,27 +421,30 @@
         row_copies[o].wait_recv()
         total_rows = total_rows + row_recv[o]
     gr_out[...] = total_rows
-    for o in reversed(range(1, n_grp)):
+    for o in (3, 2):
         x_back[o].wait_recv()
         own[...] += zrecv[o].astype(F32)
     gx_out[...] = own[...].astype(BF16)
 
-    for o in range(1, n_grp):
-        x_copies[o].wait_send()
-        y_copies[o].wait_send()
-        row_copies[o].wait_send()
-        x_back[o].wait_send()
+    for copy in far + relay + [x_back[2], x_back[3]] + row_copies[1:]:
+        copy.wait_send()
+    for h in (0, 1):
+        to_partner(h).wait_send()
+    pass_panel(0).wait_send()
 
     def finish(o, carry):
         s_copy(msend.at[o], mrecv.at[o], ms.at[o], mr.at[o], o).wait_send()
         s_copy(gsend.at[o], grecv.at[o], gs.at[o], gr.at[o], o).wait_send()
 
-        def each(stage, inner):
+        pass_panel(o).wait_send()
+
+        def each(turn, inner):
+            stage = turn + (turn + 2) // 3
             s_copy(send.at[stage, o], recv.at[stage, o], ds.at[stage, o], dr.at[stage, o], o).wait_send()
             s_copy(rsend.at[stage, o], rrecv.at[stage, o], rs.at[stage, o], rr.at[stage, o], o).wait_send()
             return inner
 
-        lax.fori_loop(0, n_grp, each, 0)
+        lax.fori_loop(0, 3, each, 0)
         return carry
 
     lax.fori_loop(1, n_seq, finish, 0)
@@ -424,7 +458,7 @@
     cap = 3 * token_count // n_seq
     slots = n_seq * cap
     _, full, hidden = w_up.shape
-    if width % 128 or cap % 16 or hidden % 256 or token_count % 128 or n_grp & (n_grp - 1) or n_seq & (n_seq - 1):
+    if width % 128 or cap % 16 or hidden % 256 or token_count % 128 or n_grp != 4 or n_seq & (n_seq - 1):
         return plain_body(
             tokens, cotangent, route_ids, route_weights, reset_steps, decay, w_up, w_down)
     experts = jnp.arange(n_seq, dtype=jnp.int32)
@@ -485,6 +519,8 @@
             dma((n_seq,)), dma((n_seq,)),
             dma((n_grp,)), dma((n_grp,)),
             dma((n_grp,)), dma((n_grp,)),
+            dma((n_seq,)), dma((n_seq,)),
+            dma((2,)), dma((2,)),
             dma((4,)),
         ],
         compiler_params=pltpu.CompilerParams(

time: 180 us -> 165 us (0.917)
  Pallas kernels: 166 us -> 151 us
    pallas_call x1, Pallas kernels: 166 us -> 151 us  [body(): pl.pallas_call(functools.partial(moe_kernel, n_grp, n_seq), out_shape=(ja...]
where the time goes in v2:
time: 165 us
  Pallas kernels  151 us (92%)
  local copies, waits for them, and re-layouts  9.31 us (6%)
  other arithmetic  3.46 us (2%)
    pallas_call x1, Pallas kernels, body(): pl.pallas_call(functools.partial(moe_kernel, n_grp, n_seq), out_shape=(ja...  151 us
    unnamed x8, local copies, waits for them, and re-layouts  7.59 us

profile of v2, /device:TPU:0, one launch (start us, length us, event | category | flops | bytes accessed | tf_op | source)
XLA Modules:
  0.0 164.7 jit_solution(13111498865014021893)
XLA Ops:
  0.6 0.7 convert_element_type.27
  1.3 0.1 pad.3.clone
  1.4 0.7 convert_bitcast_fusion
  2.1 0.7 convert_reduce_fusion
  2.7 0.2 fusion.1
  3.0 0.7 select_reduce_fusion
  3.7 0.1 broadcast_in_dim.25
  3.8 0.1 convert_element_type.28
  3.9 0.1 copy.21
  4.0 0.8 copy.19
  4.8 0.0 copy-start.1
  4.9 0.1 copy.22
  4.9 0.7 maximum_maximum_fusion.info
  5.6 0.0 copy-done.1
  5.6 151.0 %shard_map.111 = (bf16[256,640]{1,0:T(8,128)(2,1)}, f32[8,256]{1,0:T(8,128)}, bf16[2560,512]{1,0:T(8,128)(2,1)}, bf16[512,2560]{1,0:T(8,128)(2,1)}) custom-call(bf16[256,640]{1,0:T(8,128)(2,1)} %tok.1, bf16[256,640]{1,0:T(8,128)(2,1)} %cot.1, f32[8,256]{1,0:T(8,128)} %maximum_maximum_fusion.info, f32[256,2]{1,0:T(8,128)} %copy-done.1, f32[1,512]{1,0:T(1,128)} %decay.1, ...), custom_call_target="tpu_custom_call" | custom-call | tf_op jit(solution)/shard_map/pallas_call | solution.py:480
  156.6 1.3 slice_bitcast_fusion
  157.9 1.7 %copy.26 = bf16[256,640]{1,0:T(8,128)(2,1)} copy(bf16[256,640]{1,0:T(8,128)(2,1)} %get-tuple-element.16) | data formatting | bytes 655360
  159.6 0.0 copy-start
  159.6 3.6 %copy.27 = bf16[1,2560,512]{2,1,0:T(8,128)(2,1)} copy(bf16[1,2560,512]{2,1,0:T(8,128)(2,1)} %bitcast.13) | data formatting | bytes 5242880
  163.2 0.0 copy-done
  163.2 1.5 copy.28
  (3 shorter events, 0.0 us)
Async XLA Ops:
  4.8 0.8 copy-start.1
  159.6 3.6 %copy-start = (bf16[512,2560]{1,0:T(8,128)(2,1)S(1)}, bf16[512,2560]{1,0:T(8,128)(2,1)}, u32[]{:S(2)}) copy-start(bf16[512,2560]{1,0:T(8,128)(2,1)} %get-tuple-element.11) | copy-start | bytes 7864324

commit v3 on v2

--- a/solution.py
+++ b/solution.py
@@ -283,7 +283,7 @@
     for o in range(1, n_seq):
         s_copy(msend.at[o], mrecv.at[o], ms.at[o], mr.at[o], o).wait_recv()
 
-    rows = 16
+    rows = 32 if cap % 32 == 0 else 16
 
     def neurons(o, carry):
         def part(i, inner):
@@ -294,7 +294,7 @@
             gate = mrecv[o, pl.ds(here, rows), 0:1]
             reset = mrecv[o, pl.ds(here, rows), 1:2]
             leak = decay[0:1, :]
-            spikes, scales = [], []
+            waves, scales, spikes = [], [], None
             membrane = None
             for step in range(STEPS):
                 if step == 0:
@@ -305,18 +305,19 @@
                     scale = keep * leak
                     scales.append(scale)
                     membrane = scale * membrane + drive
-                spike = jax.nn.sigmoid(SHARP * (membrane - 1.0))
+                wave = jnp.tanh(0.5 * SHARP * (membrane - 1.0))
+                spike = 0.5 + 0.5 * wave
                 membrane = membrane - spike
-                spikes.append(spike)
-            rate = ((spikes[0] + spikes[1] + spikes[2] + spikes[3]) / STEPS).astype(BF16).astype(F32)
+                waves.append(wave)
+                spikes = spike if spikes is None else spikes + spike
+            rate = (spikes * (1.0 / STEPS)).astype(BF16).astype(F32)
             total = jnp.sum(rate * back, 1, keepdims=True)
             gsend[o, pl.ds(here, rows), :] = jnp.broadcast_to(total, (rows, 128))
             wgt[pl.ds(at, rows), :] = (rate * gate).astype(BF16)
-            upstream = back * gate / STEPS
+            upstream = back * gate * (1.0 / STEPS)
             d_v, d_cur = None, None
             for step in reversed(range(STEPS)):
-                spike = spikes[step]
-                slope = SHARP * spike * (1.0 - spike)
+                slope = (0.25 * SHARP) * (1.0 - waves[step] * waves[step])
                 if d_v is None:
                     d_m = upstream * slope
                     d_cur = d_m
@@ -331,44 +332,40 @@
         lax.fori_loop(0, cap // rows, part, 0)
         return carry
 
-    lax.fori_loop(0, n_seq, neurons, 0)
-
+    half = n_seq // 2
+
+    def to_partner(h):
+        part = pl.ds(h * half, half)
+        return z_copy(rsend.at[1, part], rrecv.at[1, part], es.at[h], er.at[h], 1)
+
+    def give_back(stage, h):
+        base = slice_at(stage)
+        value = nt_dot(
+            dlow[h * half * cap:(h + 1) * half * cap, :], up[pl.ds(base, width), :])
+        value = value.reshape(half, cap, width)
+        if stage == 0:
+            to_partner(h).wait_recv()
+            value = value + rrecv[1, h * half:(h + 1) * half].astype(F32)
+        rsend[stage, h * half:(h + 1) * half] = value.astype(BF16)
+
+        def go(o, inner):
+            s_copy(rsend.at[stage, o], rrecv.at[stage, o], rs.at[stage, o], rr.at[stage, o], o).start()
+            return inner
+
+        if stage == 1:
+            to_partner(h).start()
+        else:
+            lax.fori_loop(max(1, h * half), (h + 1) * half, go, 0)
+            if h == 0:
+                rrecv[stage, 0] = rsend[stage, 0]
+
+    for h in (0, 1):
+        lax.fori_loop(h * half, (h + 1) * half, neurons, 0)
+        for stage in (1, 3, 2):
+            give_back(stage, h)
     for o in range(1, n_seq):
         s_copy(gsend.at[o], grecv.at[o], gs.at[o], gr.at[o], o).start()
     grecv[0] = gsend[0]
-
-    half = n_seq // 2
-
-    def to_partner(h):
-        part = pl.ds(h * half, half)
-        return z_copy(rsend.at[1, part], rrecv.at[1, part], es.at[h], er.at[h], 1)
-
-    def give_back(stage):
-        base = slice_at(stage)
-
-        def block(h, inner):
-            at = pl.multiple_of(h * half * cap, half * cap)
-            value = nt_dot(dlow[pl.ds(at, half * cap), :], up[pl.ds(base, width), :])
-            value = value.reshape(half, cap, width)
-            if stage == 0:
-                to_partner(h).wait_recv()
-                value = value + rrecv[1, pl.ds(h * half, half)].astype(F32)
-            rsend[stage, pl.ds(h * half, half)] = value.astype(BF16)
-            if stage == 1:
-                to_partner(h).start()
-            return inner
-
-        def go(o, inner):
-            s_copy(rsend.at[stage, o], rrecv.at[stage, o], rs.at[stage, o], rr.at[stage, o], o).start()
-            return inner
-
-        lax.fori_loop(0, 2, block, 0)
-        if stage != 1:
-            rrecv[stage, 0] = rsend[stage, 0]
-            lax.fori_loop(1, n_seq, go, 0)
-
-    for stage in (1, 3, 2):
-        give_back(stage)
 
     def weight_grads(stage, carry):
         base = slice_at(stage)
@@ -379,7 +376,8 @@
         return carry
 
     lax.fori_loop(0, n_grp, weight_grads, 0)
-    give_back(0)
+    give_back(0, 0)
+    give_back(0, 1)
     store_up = pltpu.make_async_copy(gu, gu_out, local.at[2])
     store_down = pltpu.make_async_copy(gd, gd_out, local.at[3])
     store_up.start()

time: 165 us -> 168 us (1.018)
  Pallas kernels: 151 us -> 154 us
    pallas_call x1, Pallas kernels: 151 us -> 154 us  [body(): pl.pallas_call(functools.partial(moe_kernel, n_grp, n_seq), out_shape=(ja...]
where the time goes in v3:
time: 168 us; the launch traced here: 167 us
  Pallas kernels  154 us (92%)
  local copies, waits for them, and re-layouts  9.31 us (6%)
  other arithmetic  3.46 us (2%)
    pallas_call x1, Pallas kernels, body(): pl.pallas_call(functools.partial(moe_kernel, n_grp, n_seq), out_shape=(ja...  154 us
    unnamed x8, local copies, waits for them, and re-layouts  7.59 us

profile of v3, /device:TPU:0, one launch (start us, length us, event | category | flops | bytes accessed | tf_op | source)
XLA Modules:
  0.0 167.4 jit_solution(11471507019546917860)
XLA Ops:
  0.6 0.7 convert_element_type.27
  1.3 0.1 pad.3.clone
  1.4 0.7 convert_bitcast_fusion
  2.1 0.7 convert_reduce_fusion
  2.7 0.2 fusion.1
  3.0 0.7 select_reduce_fusion
  3.7 0.1 broadcast_in_dim.25
  3.8 0.1 convert_element_type.28
  3.9 0.1 copy.21
  4.0 0.8 copy.19
  4.8 0.0 copy-start.1
  4.9 0.1 copy.22
  4.9 0.7 maximum_maximum_fusion.info
  5.6 0.0 copy-done.1
  5.6 153.8 %shard_map.111 = (bf16[256,640]{1,0:T(8,128)(2,1)}, f32[8,256]{1,0:T(8,128)}, bf16[2560,512]{1,0:T(8,128)(2,1)}, bf16[512,2560]{1,0:T(8,128)(2,1)}) custom-call(bf16[256,640]{1,0:T(8,128)(2,1)} %tok.1, bf16[256,640]{1,0:T(8,128)(2,1)} %cot.1, f32[8,256]{1,0:T(8,128)} %maximum_maximum_fusion.info, f32[256,2]{1,0:T(8,128)} %copy-done.1, f32[1,512]{1,0:T(1,128)} %decay.1, ...), custom_call_target="tpu_custom_call" | custom-call | tf_op jit(solution)/shard_map/pallas_call | solution.py:478
  159.4 1.3 slice_bitcast_fusion
  160.7 1.7 %copy.26 = bf16[256,640]{1,0:T(8,128)(2,1)} copy(bf16[256,640]{1,0:T(8,128)(2,1)} %get-tuple-element.16) | data formatting | bytes 655360
  162.4 0.0 copy-start
  162.4 3.6 %copy.27 = bf16[1,2560,512]{2,1,0:T(8,128)(2,1)} copy(bf16[1,2560,512]{2,1,0:T(8,128)(2,1)} %bitcast.13) | data formatting | bytes 5242880
  165.9 0.0 copy-done
  165.9 1.5 copy.28
  (3 shorter events, 0.0 us)
Async XLA Ops:
  4.8 0.8 copy-start.1
  162.4 3.6 %copy-start = (bf16[512,2560]{1,0:T(8,128)(2,1)S(1)}, bf16[512,2560]{1,0:T(8,128)(2,1)}, u32[]{:S(2)}) copy-start(bf16[512,2560]{1,0:T(8,128)(2,1)} %get-tuple-element.11) | copy-start | bytes 7864324
